TPU v7x, 32 devices: a whole 2x2x4 slice. The times are simulated.
32 devices in a mesh: seq: 8 (over z, x), row: 4 (over y, core).
Axes of the slice: x: 2, y: 2, z: 4, core: 2. Of those that a mesh axis runs over, the one named last changes fastest.
Arguments:
- tokens: bfloat16 [4, 8192, 768], P('row', 'seq'), as said below
- doc_lengths: int32 [4, 4], P('row'), may hold values from 64 to 8000, as said below
- w_qkv: bfloat16 [768, 2304], replicated, may hold values from -0.21875 to 0.21875
- w_out: bfloat16 [768, 768], replicated, may hold values from -0.21875 to 0.21875
- conv_taps: float32 [12, 33], replicated, may hold values from -0.5 to 0.5
- norm1_gain: float32 [768], replicated, may hold values from 0.25 to 1.75
- norm1_bias: float32 [768], replicated, may hold values from -1.5 to 1.5
- w_up: bfloat16 [768, 3072], replicated, may hold values from -0.21875 to 0.21875
- w_down: bfloat16 [3072, 768], replicated, may hold values from -0.109375 to 0.109375
- norm2_gain: float32 [768], replicated, may hold values from 0.25 to 1.75
- norm2_bias: float32 [768], replicated, may hold values from -1.5 to 1.5
- cotangent: bfloat16 [4, 8192, 768], P('row', 'seq'), may hold values from -6 to 6
Outputs:
- outputs: bfloat16 [4, 8192, 768], P('row', 'seq')
- grad_tokens: float32 [4, 8192, 768], P('row', 'seq')
- grad_w_qkv: float32 [768, 2304], replicated
- grad_w_out: float32 [768, 768], replicated
- grad_conv_taps: float32 [12, 33], replicated
- grad_norm1_gain: float32 [768], replicated
- grad_norm1_bias: float32 [768], replicated
- grad_w_up: float32 [768, 3072], replicated
- grad_w_down: float32 [3072, 768], replicated
- grad_norm2_gain: float32 [768], replicated
- grad_norm2_bias: float32 [768], replicated
Inputs may be any that keep to these rules, and one draw needn't show every extreme that they name: `tokens`: activations of the previous layer. `doc_lengths`: each row's 4 lengths sum to 8192; every document holds at least 64 tokens, and one of them more than 7168.
All inputs are finite; a program needn't handle non-finite values.
Results may differ from a plain program's by a relative error of at most 0.014.
Values may be sent and summed in bfloat16 or wider, within the bound.
A program may use at most 320 MiB of HBM per device.

v0:
```python
import jax
import jax.numpy as jnp
from jax import lax
from jax.sharding import PartitionSpec as P

LMK = 64
NS_ITERS = 6
DOCS = 4


HIGHEST = lax.Precision.HIGHEST
EPSILON = 1e-05
BIG_NEGATIVE = -1e30


def extended(x, sides, width):
    for axis, dim in sides:
        count, length = (lax.axis_size(axis), x.shape[dim])
        up = [(i, (i + 1) % count) for i in range(count - 1)]
        down = [(j, i) for i, j in up]
        last = lax.slice_in_dim(x, length - width, length, axis=dim)
        first = lax.slice_in_dim(x, 0, width, axis=dim)
        before = lax.ppermute(last, axis, up)
        after = lax.ppermute(first, axis, down)
        x = jnp.concatenate([before, x, after], axis=dim)
    return x


def layout(lengths, places):
    doc_end = jnp.cumsum(lengths)
    doc_starts = doc_end - lengths
    doc_ids = jnp.sum((places[:, None] >= doc_starts[None, :]).astype(jnp.int32), axis=1) - 1
    chosen = (doc_ids[:, None] == jnp.arange(DOCS, dtype=jnp.int32)[None, :]).astype(jnp.int32)
    doc_length = jnp.sum(chosen * lengths[None, :], axis=1)
    doc_start = jnp.sum(chosen * doc_starts[None, :], axis=1)
    segment = (places - doc_start) * LMK // jnp.maximum(doc_length, 1)
    return (doc_ids, doc_ids * LMK + segment)


def slot_counts(lengths):
    mark_ids = jnp.arange(DOCS * LMK, dtype=jnp.int32)
    which_doc = mark_ids // LMK
    within = mark_ids % LMK
    chosen = (which_doc[:, None] == jnp.arange(DOCS, dtype=jnp.int32)[None, :]).astype(jnp.int32)
    doc_length = jnp.sum(chosen * lengths[None, :], axis=1)
    upper = ((within + 1) * doc_length + LMK - 1) // LMK
    lower = (within * doc_length + LMK - 1) // LMK
    return (upper - lower).astype(jnp.float32)


def layer_norm(inputs, gain, bias):
    average = jnp.mean(inputs, axis=-1, keepdims=True)
    centered = inputs - average
    variance = jnp.mean(centered * centered, axis=-1, keepdims=True)
    return centered * lax.rsqrt(variance + EPSILON) * gain + bias


def gelu(inputs):
    return 0.5 * inputs * (1.0 + lax.erf(inputs * 0.7071067811865476))


def masked_softmax(scores, allowed):
    highest = jnp.max(jnp.where(allowed, scores, BIG_NEGATIVE), axis=-1, keepdims=True)
    exponent = jnp.exp(jnp.where(allowed, scores - highest, BIG_NEGATIVE))
    return exponent / jnp.sum(exponent, axis=-1, keepdims=True)


def inverse_from_scores(scores):
    highest = jnp.max(scores, axis=-1, keepdims=True)
    exponent = jnp.exp(scores - highest)
    kernel_a = exponent / jnp.sum(exponent, axis=-1, keepdims=True)
    scale = jnp.sum(kernel_a * kernel_a, axis=(2, 3), keepdims=True)
    approx = jnp.swapaxes(kernel_a, 2, 3) / scale
    identity = jnp.eye(LMK, dtype=jnp.float32)
    for sweep in range(NS_ITERS):
        product = jnp.einsum("dhlm,dhmn->dhln", kernel_a, approx, precision=HIGHEST)
        bracket = 7.0 * identity - product
        bracket = 15.0 * identity - jnp.einsum(
            "dhlm,dhmn->dhln", product, bracket, precision=HIGHEST
        )
        bracket = 13.0 * identity - jnp.einsum(
            "dhlm,dhmn->dhln", product, bracket, precision=HIGHEST
        )
        approx = 0.25 * jnp.einsum("dhlm,dhmn->dhln", approx, bracket, precision=HIGHEST)
    return approx


def split_heads(matrix, head_count):
    return matrix.reshape(matrix.shape[0], head_count, matrix.shape[1] // head_count)


def on_device(
    tokens,
    doc_lengths,
    w_qkv,
    w_out,
    conv_taps,
    norm1_gain,
    norm1_bias,
    w_up,
    w_down,
    norm2_gain,
    norm2_bias,
    cotangent,
):
    shard_len = tokens.shape[1]
    model_width = tokens.shape[2]
    head_count = conv_taps.shape[0]
    tap_count = conv_taps.shape[1]
    head_width = model_width // head_count
    slot_count = DOCS * LMK
    rim_width = (tap_count - 1) // 2
    shard_start = lax.axis_index("seq") * shard_len
    lengths = doc_lengths[0]
    doc_ids, slot_ids = layout(lengths, shard_start + jnp.arange(shard_len, dtype=jnp.int32))
    around_ids = layout(
        lengths, shard_start - rim_width + jnp.arange(shard_len + 2 * rim_width, dtype=jnp.int32)
    )[0]
    counts = slot_counts(lengths)
    mark_doc = jnp.arange(slot_count, dtype=jnp.int32) // LMK
    inputs = tokens[0]
    joined = jnp.dot(inputs, w_qkv, preferred_element_type=jnp.float32).astype(jnp.bfloat16)
    queries = joined[:, :model_width]
    key_rows = joined[:, model_width : 2 * model_width]
    values = joined[:, 2 * model_width :]
    member = (slot_ids[None, :] == jnp.arange(slot_count, dtype=jnp.int32)[:, None]).astype(
        jnp.bfloat16
    )
    partial_sums = jnp.dot(member, joined[:, : 2 * model_width], preferred_element_type=jnp.float32)
    landmark_sums = lax.psum(partial_sums, "seq")
    landmarks = (landmark_sums / counts[:, None]).astype(jnp.bfloat16)
    query_marks = landmarks[:, :model_width]
    key_marks = landmarks[:, model_width:]
    query_docs = query_marks.reshape(DOCS, LMK, head_count, head_width)
    key_docs = key_marks.reshape(DOCS, LMK, head_count, head_width)
    mark_scores = (
        jnp.einsum("dlhe,dmhe->dhlm", query_docs, key_docs, preferred_element_type=jnp.float32)
        * 0.125
    )
    approx, inverse_pull = jax.vjp(inverse_from_scores, mark_scores)
    qm_heads = split_heads(query_marks, head_count)
    km_heads = split_heads(key_marks, head_count)
    query_heads = split_heads(queries, head_count)
    key_heads = split_heads(key_rows, head_count)
    value_heads = split_heads(values, head_count)
    key_allowed = (mark_doc[:, None] == doc_ids[None, :])[None]
    scores_b = (
        jnp.einsum("she,the->hst", qm_heads, key_heads, preferred_element_type=jnp.float32) * 0.125
    )
    maxima = lax.pmax(jnp.max(jnp.where(key_allowed, scores_b, BIG_NEGATIVE), axis=2), "seq")
    exponent = jnp.exp(jnp.where(key_allowed, scores_b - maxima[:, :, None], BIG_NEGATIVE))
    weights_b = exponent.astype(jnp.bfloat16)
    weighted_part = jnp.einsum(
        "hst,the->she", weights_b, value_heads, preferred_element_type=jnp.float32
    )
    denominator, weighted = lax.psum((jnp.sum(exponent, axis=2), weighted_part), "seq")
    mixed_values = weighted / jnp.transpose(denominator)[:, :, None]
    mixed_docs = mixed_values.reshape(DOCS, LMK, head_count, -1)
    carried = (
        jnp.einsum("dhlm,dmhe->dlhe", approx, mixed_docs, precision=HIGHEST)
        .reshape(slot_count, head_count, -1)
        .astype(jnp.bfloat16)
    )
    query_allowed = (doc_ids[:, None] == mark_doc[None, :])[:, None, :]
    scores_f = (
        jnp.einsum("the,she->ths", query_heads, km_heads, preferred_element_type=jnp.float32)
        * 0.125
    )
    kernel = masked_softmax(scores_f, query_allowed)
    kernel_b = kernel.astype(jnp.bfloat16)
    attended = jnp.einsum(
        "ths,she->the", kernel_b, carried, preferred_element_type=jnp.float32
    ).reshape(shard_len, model_width)
    tap_table = jnp.repeat(jnp.transpose(conv_taps), head_width, axis=1)
    padded = extended(values, (("seq", 0),), rim_width)
    convolved = jnp.zeros((shard_len, model_width), jnp.float32)
    for tap_index in range(tap_count):
        same_doc = (around_ids[tap_index : tap_index + shard_len] == doc_ids)[:, None]
        convolved = convolved + jnp.where(
            same_doc,
            tap_table[tap_index] * padded[tap_index : tap_index + shard_len].astype(jnp.float32),
            0.0,
        )
    mixture_b = (attended + convolved).astype(jnp.bfloat16)
    residual1 = inputs.astype(jnp.float32) + jnp.dot(
        mixture_b, w_out, preferred_element_type=jnp.float32
    )
    normed1, norm1_pull = jax.vjp(layer_norm, residual1, norm1_gain, norm1_bias)
    normed1_b = normed1.astype(jnp.bfloat16)
    upward = jnp.dot(normed1_b, w_up, preferred_element_type=jnp.float32)
    activated_wide, gelu_pull = jax.vjp(gelu, upward)
    activated = activated_wide.astype(jnp.bfloat16)
    residual2 = normed1 + jnp.dot(activated, w_down, preferred_element_type=jnp.float32)
    result, norm2_pull = jax.vjp(layer_norm, residual2, norm2_gain, norm2_bias)
    delta_residual2, delta_gain2, delta_bias2 = norm2_pull(cotangent[0].astype(jnp.float32))
    delta_down = delta_residual2.astype(jnp.bfloat16)
    grad_down = jnp.dot(activated.T, delta_down, preferred_element_type=jnp.float32)
    delta_active = jnp.dot(delta_down, w_down.T, preferred_element_type=jnp.float32)
    delta_up = gelu_pull(delta_active)[0].astype(jnp.bfloat16)
    grad_up = jnp.dot(normed1_b.T, delta_up, preferred_element_type=jnp.float32)
    delta_normed1 = delta_residual2 + jnp.dot(delta_up, w_up.T, preferred_element_type=jnp.float32)
    delta_residual1, delta_gain1, delta_bias1 = norm1_pull(delta_normed1)
    delta_output = delta_residual1.astype(jnp.bfloat16)
    grad_output = jnp.dot(mixture_b.T, delta_output, preferred_element_type=jnp.float32)
    delta_mixture = jnp.dot(delta_output, w_out.T, preferred_element_type=jnp.float32)
    delta_padded = extended(delta_mixture.astype(jnp.bfloat16), (("seq", 0),), rim_width).astype(
        delta_mixture.dtype
    )
    delta_conv_values = jnp.zeros((shard_len, model_width), jnp.float32)
    tap_terms = []
    for tap_index in range(tap_count):
        same_doc = (around_ids[tap_index : tap_index + shard_len] == doc_ids)[:, None]
        mirror = 2 * rim_width - tap_index
        same_back = (around_ids[mirror : mirror + shard_len] == doc_ids)[:, None]
        delta_conv_values = delta_conv_values + jnp.where(
            same_back, tap_table[tap_index] * delta_padded[mirror : mirror + shard_len], 0.0
        )
        tap_terms.append(
            jnp.sum(
                jnp.where(
                    same_doc,
                    delta_mixture * padded[tap_index : tap_index + shard_len].astype(jnp.float32),
                    0.0,
                ),
                axis=0,
            )
        )
    grad_taps = jnp.transpose(
        jnp.sum(jnp.stack(tap_terms).reshape(tap_count, head_count, -1), axis=2)
    )
    delta_attended = split_heads(delta_mixture.astype(jnp.bfloat16), head_count)
    carried_part = jnp.einsum(
        "ths,the->she", kernel_b, delta_attended, preferred_element_type=jnp.float32
    )
    delta_kernel = jnp.einsum(
        "the,she->ths", delta_attended, carried, preferred_element_type=jnp.float32
    )
    delta_scores_f = (
        kernel * (delta_kernel - jnp.sum(kernel * delta_kernel, axis=2, keepdims=True))
    ).astype(jnp.bfloat16)
    delta_queries_f = (
        jnp.einsum("ths,she->the", delta_scores_f, km_heads, preferred_element_type=jnp.float32)
        * 0.125
    )
    keymark_part = (
        jnp.einsum("ths,the->she", delta_scores_f, query_heads, preferred_element_type=jnp.float32)
        * 0.125
    )
    delta_carried, delta_keymarks_f = lax.psum(
        (carried_part, keymark_part.reshape(slot_count, model_width)), "seq"
    )
    delta_carried_docs = delta_carried.reshape(DOCS, LMK, head_count, -1)
    delta_approx = jnp.einsum("dlhe,dmhe->dhlm", delta_carried_docs, mixed_docs, precision=HIGHEST)
    delta_mixed = jnp.einsum(
        "dhlm,dlhe->dmhe", approx, delta_carried_docs, precision=HIGHEST
    ).reshape(slot_count, head_count, -1)
    delta_mark_scores = inverse_pull(delta_approx)[0]
    key_docs_wide = key_docs.astype(jnp.float32)
    query_docs_wide = query_docs.astype(jnp.float32)
    delta_querymarks_a = (
        jnp.einsum("dhlm,dmhe->dlhe", delta_mark_scores, key_docs_wide, precision=HIGHEST) * 0.125
    ).reshape(slot_count, model_width)
    delta_keymarks_a = (
        jnp.einsum("dhlm,dlhe->dmhe", delta_mark_scores, query_docs_wide, precision=HIGHEST) * 0.125
    ).reshape(slot_count, model_width)
    scaled_grad = delta_mixed / jnp.transpose(denominator)[:, :, None]
    upper_part = scaled_grad.astype(jnp.bfloat16)
    lower_part = (scaled_grad - upper_part.astype(jnp.float32)).astype(jnp.bfloat16)
    delta_values_b = jnp.einsum(
        "hst,she->the", weights_b, upper_part, preferred_element_type=jnp.float32
    ) + jnp.einsum("hst,she->the", weights_b, lower_part, preferred_element_type=jnp.float32)
    along_values = jnp.einsum(
        "the,she->hst", value_heads, upper_part, preferred_element_type=jnp.float32
    ) + jnp.einsum("the,she->hst", value_heads, lower_part, preferred_element_type=jnp.float32)
    along_mixed = jnp.transpose(jnp.sum(scaled_grad * mixed_values, axis=2))
    delta_scores_b = (exponent * (along_values - along_mixed[:, :, None])).astype(jnp.bfloat16)
    delta_keys_b = (
        jnp.einsum("hst,she->the", delta_scores_b, qm_heads, preferred_element_type=jnp.float32)
        * 0.125
    )
    querymark_part = (
        jnp.einsum("hst,the->she", delta_scores_b, key_heads, preferred_element_type=jnp.float32)
        * 0.125
    )
    delta_querymarks_b = lax.psum(querymark_part.reshape(slot_count, model_width), "seq")
    delta_query_sums = ((delta_querymarks_a + delta_querymarks_b) / counts[:, None]).astype(
        jnp.bfloat16
    )
    delta_key_sums = ((delta_keymarks_a + delta_keymarks_f) / counts[:, None]).astype(jnp.bfloat16)
    from_marks = jnp.dot(
        member.T,
        jnp.concatenate([delta_query_sums, delta_key_sums], axis=1),
        preferred_element_type=jnp.float32,
    )
    delta_joined = jnp.concatenate(
        [
            delta_queries_f.reshape(shard_len, model_width) + from_marks[:, :model_width],
            delta_keys_b.reshape(shard_len, model_width) + from_marks[:, model_width:],
            delta_values_b.reshape(shard_len, model_width) + delta_conv_values,
        ],
        axis=1,
    ).astype(jnp.bfloat16)
    grad_joined = jnp.dot(inputs.T, delta_joined, preferred_element_type=jnp.float32)
    delta_inputs = delta_residual1 + jnp.dot(
        delta_joined, w_qkv.T, preferred_element_type=jnp.float32
    )
    norm_terms = jnp.stack([delta_gain1, delta_bias1, delta_gain2, delta_bias2])
    taps_total, norms_total = lax.psum((grad_taps, norm_terms), ("seq", "row"))
    groups = lax.axis_size(("seq", "row"))
    summed = (
        lax.psum_scatter(
            grad_joined.reshape(groups, -1), ("seq", "row"), scatter_dimension=0, tiled=True
        ),
        lax.psum_scatter(
            grad_output.reshape(groups, -1), ("seq", "row"), scatter_dimension=0, tiled=True
        ),
        lax.psum_scatter(
            grad_up.reshape(groups, -1), ("seq", "row"), scatter_dimension=0, tiled=True
        ),
        lax.psum_scatter(
            grad_down.reshape(groups, -1), ("seq", "row"), scatter_dimension=0, tiled=True
        ),
    )
    gathered = (
        lax.all_gather(summed[0].astype(jnp.bfloat16), ("seq", "row"), axis=0, tiled=True).astype(
            jnp.float32
        ),
        lax.all_gather(summed[1].astype(jnp.bfloat16), ("seq", "row"), axis=0, tiled=True).astype(
            jnp.float32
        ),
        lax.all_gather(summed[2].astype(jnp.bfloat16), ("seq", "row"), axis=0, tiled=True).astype(
            jnp.float32
        ),
        lax.all_gather(summed[3].astype(jnp.bfloat16), ("seq", "row"), axis=0, tiled=True).astype(
            jnp.float32
        ),
    )
    return (
        result.astype(jnp.bfloat16)[None],
        delta_inputs[None],
        gathered[0].reshape(grad_joined.shape),
        gathered[1].reshape(grad_output.shape),
        taps_total,
        norms_total[0],
        norms_total[1],
        gathered[2].reshape(grad_up.shape),
        gathered[3].reshape(grad_down.shape),
        norms_total[2],
        norms_total[3],
    )


def solution(mesh):
    return jax.shard_map(
        on_device,
        mesh=mesh,
        in_specs=(
            P("row", "seq", None),
            P("row", None),
            P(),
            P(),
            P(),
            P(),
            P(),
            P(),
            P(),
            P(),
            P(),
            P("row", "seq", None),
        ),
        out_specs=(
            P("row", "seq", None),
            P("row", "seq", None),
            P(),
            P(),
            P(),
            P(),
            P(),
            P(),
            P(),
            P(),
            P(),
        ),
        check_vma=False,
    )
```

profile of v0, /device:TPU:0, one launch (start us, length us, event | category | flops | bytes accessed | tf_op | source)
XLA Modules:
  0.0 1955.9 jit_solution(584431181103678871)
XLA Ops:
  104.0 17.4 all-reduce.12.cloned.1.call-done
  207.7 35.5 %pmax.7 = f32[12,256]{1,0:T(8,128)S(1)} all-reduce(f32[12,256]{1,0:T(8,128)} %get-tuple-element.201), channel_id=1, replica_groups=mesh['seq'=8,'row'=4] {'seq'}, use_global_device_ids=true, to_apply=%region_7.8 | all-reduce | flops 3072 | bytes 24576 | tf_op jit(solution)/shard_map/pmax | solution.py:150
  243.3 10.4 fusion.8
  253.7 33.3 %psum.58 = f32[256,12]{0,1:T(8,128)S(1)} all-reduce(f32[256,12]{0,1:T(8,128)} %bitcast.334), channel_id=1, replica_groups=mesh['seq'=8,'row'=4] {'seq'}, use_global_device_ids=true, to_apply=%region_10.11 | all-reduce | flops 3072 | bytes 24576 | tf_op jit(solution)/shard_map/psum | solution.py:156
  293.2 11.9 fusion.387
  305.1 60.2 %all-reduce.14.cloned.1.call-done = f32[256,12,64]{0,2,1:T(8,128)} async-done(((f32[256,12,64]{0,2,1:T(8,128)}), f32[256,12,64]{0,2,1:T(8,128)}) %all-reduce.14.cloned.1.call-update) | async-done | bytes 786448 | tf_op jit(solution)/shard_map/psum | solution.py:156
  392.5 59.0 %fusion.127 = bf16[1024,768]{1,0:T(8,128)(2,1)} fusion(f32[1024,768]{1,0:T(8,128)} %copy.233, bf16[1024,768]{1,0:T(8,128)(2,1)} %get-tuple-element.156, bf16[16,768]{1,0:T(8,128)(2,1)} %collective-permute-done.1, bf16[16,768]{1,0:T(8,128)(2,1)} %collective-permute-done, f32[768]{0:T(1024)} %broadcast_in_dim.924, f32[768]{0:T(1024)} %broadcast_in_dim.921, ...), kind=kLoop, calls=%fused_computation.244 | loop fusion | flops 180092928 | bytes 6475776 | tf_op jit(solution)/shard_map/convert_element_type | solution.py:184
  456.2 12.4 multiply_convert_fusion.1
  480.4 11.2 fusion.338
  491.5 12.9 add_convert_fusion
  504.5 8.8 multiply_reduce_fusion
  513.3 10.7 fusion.369
  546.1 9.0 fusion.1
  570.4 10.7 fusion.150
  591.3 8.4 fusion.65
  627.9 8.4 fusion.89
  645.7 9.6 fusion.116
  656.6 10.2 fusion.104
  762.1 15.5 all-reduce.16.cloned.1.call-done
  952.2 11.5 multiply_convert_fusion
  969.4 60.0 %fusion.155 = bf16[1024,768]{1,0:T(8,128)(2,1)} fusion(f32[1024,768]{1,0:T(8,128)} %copy.272, f32[1056,768]{1,0:T(8,128)} %maximum_convert_fusion, f32[768]{0:T(1024)} %broadcast_in_dim.924, f32[768]{0:T(1024)} %broadcast_in_dim.921, f32[768]{0:T(1024)} %broadcast_in_dim.918, f32[768]{0:T(1024)} %broadcast_in_dim.915, f32[768]{0:T(1024)} %broadcast_in_dim.912, ...), kind=kLoop, calls=%fused_computation.273 | loop fusion | flops 78643200 | bytes 108662784 | tf_op jit(solution)/shard_map/convert.6
  1061.3 57.1 %all-reduce.18.cloned.1.call-done = (f32[256,768]{0,1:T(8,128)}, f32[256,768]{0,1:T(8,128)}) async-done(((f32[256,768]{0,1:T(8,128)}, f32[256,768]{0,1:T(8,128)}), (f32[256,768]{0,1:T(8,128)}, f32[256,768]{0,1:T(8,128)})) %all-reduce.18.cloned.1.call-update) | async-done | bytes 1572880 | tf_op jit(solution)/shard_map/psum | solution.py:249
  1147.6 459.2 %all-reduce.19 = (bf16[32,55296]{1,0:T(8,128)(2,1)}, bf16[32,18432]{1,0:T(8,128)(2,1)}, f32[12,33]{0,1:T(8,128)}, f32[4,768]{1,0:T(4,128)}, bf16[32,73728]{1,0:T(8,128)(2,1)}, /*index=5*/bf16[32,73728]{1,0:T(8,128)(2,1)}) all-reduce(f32[32,55296]{1,0:T(8,128)} %reshape.661, ...), channel_id=2, replica_groups=mesh['seq'=8,'row'=4] {'seq','row'}, use_global_device_ids=true, to_apply=%region_34.35.clone | all-reduce | flops 7081356 | bytes 42495072
  1618.1 8.8 add_bitcast_fusion
  1632.6 32.5 %all-gather.11.cloned.1.call-done = bf16[32,1,18432]{2,1,0:T(2,128)(2,1)} async-done(((bf16[1,1,18432]{2,1,0:T(2,128)(2,1)}), bf16[32,1,18432]{2,1,0:T(2,128)(2,1)}) %all-gather.11.cloned.1.call-update) | async-done | bytes 1179664 | tf_op jit(solution)/shard_map/all_gather | solution.py:328
  1665.0 9.7 convert_reduce_fusion.4
  1677.7 62.1 %all-gather.9.cloned.1.call-done = bf16[32,1,55296]{2,1,0:T(2,128)(2,1)} async-done(((bf16[1,1,55296]{2,1,0:T(2,128)(2,1)}), bf16[32,1,55296]{2,1,0:T(2,128)(2,1)}) %all-gather.9.cloned.1.call-update) | async-done | bytes 3538960 | tf_op jit(solution)/shard_map/all_gather | solution.py:325
  1739.8 65.8 %convert_reduce_fusion.2 = f32[32,55296]{1,0:T(8,128)} fusion(bf16[32,1,55296]{2,1,0:T(2,128)(2,1)} %all-gather.9.cloned.1.call-done), kind=kLoop, calls=%fused_computation.50 | loop fusion | flops 1769472 | bytes 10616832 | tf_op jit(solution)/shard_map/reshape | solution.py:341
  1812.2 12.1 all-gather.15.cloned.1.call-done
  1824.3 32.2 %convert_reduce_fusion = f32[32,73728]{1,0:T(8,128)} fusion(bf16[32,1,73728]{2,1,0:T(2,128)(2,1)} %all-gather.15.cloned.1.call-done), kind=kLoop, calls=%fused_computation.48 | loop fusion | flops 2359296 | bytes 14155776 | tf_op jit(solution)/shard_map/reshape | solution.py:347
  1864.5 43.8 %all-gather.13.cloned.1.call-done = bf16[32,1,73728]{2,1,0:T(2,128)(2,1)} async-done(((bf16[1,1,73728]{2,1,0:T(2,128)(2,1)}), bf16[32,1,73728]{2,1,0:T(2,128)(2,1)}) %all-gather.13.cloned.1.call-update) | async-done | bytes 4718608 | tf_op jit(solution)/shard_map/all_gather | solution.py:331
  1908.3 32.1 %convert_reduce_fusion.1 = f32[32,73728]{1,0:T(8,128)} fusion(bf16[32,1,73728]{2,1,0:T(2,128)(2,1)} %all-gather.13.cloned.1.call-done), kind=kLoop, calls=%fused_computation.49 | loop fusion | flops 2359296 | bytes 14155776 | tf_op jit(solution)/shard_map/reshape | solution.py:346
  (666 shorter events, 696.7 us)
Async XLA Ops:
  7.2 17.4 copy-start.140
  7.2 114.3 %all-reduce.12.cloned.1.call-start = ((), (), s32[]{:S(2)}) async-start(), calls=%async_computation | async-start | bytes 3145728 | tf_op jit(solution)/shard_map/psum | solution.py:130
  17.9 374.6 %collective-permute-start = (bf16[16,768]{1,0:T(8,128)(2,1)}, bf16[16,768]{1,0:T(8,128)(2,1)}, u32[]{:S(2)}, u32[]{:S(2)}) collective-permute-start(bf16[16,768]{1,0:T(8,128)(2,1)} %get-tuple-element.152), channel_id=1, source_target_pairs={{0,4},{4,8},{8,12},{12,16},{16,20},{20,24},{24,28},{1,5},{5,9},{9,... | collective-permute-start | bytes 73736 | tf_op jit(solution)/shard_map/ppermute | solution.py:23
  23.3 369.2 %collective-permute-start.1 = (bf16[16,768]{1,0:T(8,128)(2,1)}, bf16[16,768]{1,0:T(8,128)(2,1)}, u32[]{:S(2)}, u32[]{:S(2)}) collective-permute-start(bf16[16,768]{1,0:T(8,128)(2,1)} %get-tuple-element.153), channel_id=1, source_target_pairs={{4,0},{8,4},{12,8},{16,12},{20,16},{24,20},{28,24},{5,1},{9,5},{13... | collective-permute-start | bytes 73736 | tf_op jit(solution)/shard_map/ppermute | solution.py:24
  29.9 335.4 %all-reduce.14.cloned.1.call-start = ((), (), s32[]{:S(2)}) async-start(), calls=%async_computation.1 | async-start | bytes 1572864 | tf_op jit(solution)/shard_map/psum | solution.py:156
  100.7 23.3 %copy-start.122 = (f32[256]{0:T(256)}, f32[256]{0:T(256)S(1)}, u32[]{:S(2)}) copy-start(f32[256]{0:T(256)S(1)} %subtract_convert_fusion.1) | copy-start | bytes 3076
  135.0 55.5 %copy-start.19 = (f32[4,12,64,64]{2,3,1,0:T(8,128)}, f32[4,12,64,64]{2,3,1,0:T(8,128)S(1)}, u32[]{:S(2)}) copy-start(f32[4,12,64,64]{2,3,1,0:T(8,128)S(1)} %get-tuple-element.204) | copy-start | bytes 2359300
  135.0 55.5 %copy-start.95 = (f32[4,12,64]{2,1,0:T(8,128)}, f32[4,12,64]{2,1,0:T(8,128)S(1)}, u32[]{:S(2)}) copy-start(f32[4,12,64]{2,1,0:T(8,128)S(1)} %get-tuple-element.203) | copy-start | bytes 36868
  137.1 53.4 %copy-start.98 = (f32[4,12,64]{2,1,0:T(8,128)}, f32[4,12,64]{2,1,0:T(8,128)S(1)}, u32[]{:S(2)}) copy-start(f32[4,12,64]{2,1,0:T(8,128)S(1)} %get-tuple-element.159) | copy-start | bytes 36868
  243.3 10.4 copy-start.103
  287.0 78.3 %copy-start.93 = (f32[256,12]{0,1:T(8,128)}, f32[256,12]{0,1:T(8,128)S(1)}, u32[]{:S(2)}) copy-start(f32[256,12]{0,1:T(8,128)S(1)} %psum.58) | copy-start | bytes 36868
  293.2 484.3 %all-reduce.16.cloned.1.call-start = ((), (), s32[]{:S(2)}) async-start(), calls=%async_computation.2 | async-start | bytes 3145728 | tf_op jit(solution)/shard_map/psum | solution.py:249
  451.5 17.1 slice-start.5
  456.2 12.4 slice-start.6
  480.4 24.1 %slice-start.7 = ((s8[4718592]{0:T(1024)(128)(4,1)}), s8[4194304]{0:T(1024)(128)(4,1)S(1)}, s32[]{:S(2)}) async-start(s8[4718592]{0:T(1024)(128)(4,1)} %bitcast.339), calls=%async_computation.15 | async-start | bytes 8388608
  491.5 12.9 slice-start.8
  524.9 8.7 copy-start.79
  524.9 8.7 copy-start.136
  538.0 8.1 copy-start.101
  538.0 8.1 copy-start.108
  538.0 17.1 slice-start.2
  538.0 17.1 slice-start.3
  546.1 9.0 slice-start.4
  676.2 82.5 %collective-permute-start.2 = (bf16[16,768]{1,0:T(8,128)(2,1)}, bf16[16,768]{1,0:T(8,128)(2,1)}, u32[]{:S(2)}, u32[]{:S(2)}) collective-permute-start(bf16[16,768]{1,0:T(8,128)(2,1)} %get-tuple-element.160), channel_id=1, source_target_pairs={{0,4},{4,8},{8,12},{12,16},{16,20},{20,24},{24,28},{1,5},{5,9},{9,... | collective-permute-start | bytes 73736 | tf_op jit(solution)/shard_map/ppermute | solution.py:23
  679.3 79.4 %collective-permute-start.3 = (bf16[16,768]{1,0:T(8,128)(2,1)}, bf16[16,768]{1,0:T(8,128)(2,1)}, u32[]{:S(2)}, u32[]{:S(2)}) collective-permute-start(bf16[16,768]{1,0:T(8,128)(2,1)} %get-tuple-element.161), channel_id=1, source_target_pairs={{4,0},{8,4},{12,8},{16,12},{20,16},{24,20},{28,24},{5,1},{9,5},{13... | collective-permute-start | bytes 73736 | tf_op jit(solution)/shard_map/ppermute | solution.py:24
  687.3 431.0 %all-reduce.18.cloned.1.call-start = ((), (), s32[]{:S(2)}) async-start(), calls=%async_computation.7 | async-start | bytes 3145728 | tf_op jit(solution)/shard_map/psum | solution.py:249
  952.2 14.2 copy-start.59
  1029.4 635.6 %all-gather.11.cloned.1.call-start = ((), (), s32[]{:S(2)}) async-start(), calls=%async_computation.4 | async-start | bytes 2433024 | tf_op jit(solution)/shard_map/all_gather | solution.py:328
  1057.7 60.6 %copy-start.123 = (f32[256]{0:T(256)S(1)}, f32[256]{0:T(256)}, u32[]{:S(2)}) copy-start(f32[256]{0:T(256)} %copy-done.122) | copy-start | bytes 3076
  1608.4 131.3 %all-gather.9.cloned.1.call-start = ((), (), s32[]{:S(2)}) async-start(), calls=%async_computation.3 | async-start | bytes 7299072 | tf_op jit(solution)/shard_map/all_gather | solution.py:325
  1610.6 213.7 %all-gather.15.cloned.1.call-start = ((), (), s32[]{:S(2)}) async-start(), calls=%async_computation.6 | async-start | bytes 9732096 | tf_op jit(solution)/shard_map/all_gather | solution.py:334
  1613.0 295.4 %all-gather.13.cloned.1.call-start = ((), (), s32[]{:S(2)}) async-start(), calls=%async_computation.5 | async-start | bytes 9732096 | tf_op jit(solution)/shard_map/all_gather | solution.py:331
  (133 other events, 412.5 us)
Sparse Core Ops, SparseCore 0:
  30.0 91.3 all-reduce.11
  293.3 71.9 all-reduce.13
  687.4 90.0 all-reduce.15
  1029.6 88.7 all-reduce.17
  1608.6 56.4 all-gather.10
  1668.2 71.5 all-gather.8
  1743.7 80.5 all-gather.14
  1827.6 80.6 all-gather.12
where the time goes:
time: 1970 us; the launch traced here: 1960 us
  blocking collectives  528 us (27%)
  matrix products  411 us (21%)
  other arithmetic  375 us (19%)
  local copies, waits for them, and re-layouts  313 us (16%)
  waiting for transfers between devices  301 us (15%)
    unnamed x1, blocking collectives  459 us
    dot_general x36, matrix products, inverse_from_scores(): jnp.einsum('dhlm,dhmn->dhln', product, bracket, precision=HIGHEST)  90.6 us
    unnamed x347, local copies, waits for them, and re-layouts  86.8 us
    psum x2, waiting for transfers between devices, on_device(): lax.psum((carried_part, keymark_part.reshape(slot_count, model_width)), '...  72.5 us
    reshape x1, other arithmetic, on_device(): gathered[0].reshape(grad_joined.shape)  65.8 us
    reduce_sum x7, other arithmetic, on_device(): jnp.sum(jnp.where(same_doc, delta_mixture * padded[tap_index:tap_index +...  63.4 us
    all_gather x1, waiting for transfers between devices, on_device(): lax.all_gather(summed[0].astype(jnp.bfloat16), ('seq', 'row'), axis=0, ti...  62.1 us
    another operation x3, other arithmetic  61.3 us
  transfers between devices with their start and end apart: 12, of which 8 were waited for; matrix products, arithmetic and copies ran while one was open for 24% of the time, Pallas kernels for 0%

commit v1 on v0

--- a/solution.py
+++ b/solution.py
@@ -1,7 +1,13 @@
+import functools
+
 import jax
 import jax.numpy as jnp
 from jax import lax
+from jax.experimental import pallas as pl
+from jax.experimental.pallas import tpu as pltpu
 from jax.sharding import PartitionSpec as P
+
+MESH = pl.DeviceIdType.MESH
 
 LMK = 64
 NS_ITERS = 6
@@ -87,6 +93,184 @@
 
 def split_heads(matrix, head_count):
     return matrix.reshape(matrix.shape[0], head_count, matrix.shape[1] // head_count)
+
+
+def wsum_kernel(dims, gq, go, gu, gd, sm, oq, oo, ou, od, osm, own, out, r0, r1, r2, r3, smr, lsem, osem, ss, rs, sss, srs):
+    s_ax, r_ax = lax.axis_index("seq"), lax.axis_index("row")
+    z, x, y, c = s_ax // 2, s_ax % 2, r_ax // 2, r_ax % 2
+    x1, y1 = x + (1 - c) * (1 - 2 * x), y + c * (1 - 2 * y)
+    x2, y2 = x + c * (1 - 2 * x), y + (1 - c) * (1 - 2 * y)
+    core_dev = (s_ax, y * 2 + (1 - c))
+    d1_dev = (z * 2 + x1, y1 * 2 + c)
+    d2_dev = (z * 2 + x2, y2 * 2 + c)
+    z_devs = [(lax.rem(z + k, 4) * 2 + x, r_ax) for k in (1, 2, 3)]
+    peers = [core_dev, d1_dev, d2_dev] + z_devs
+    b1 = x * (1 - c) + y * c
+    b2 = y * (1 - c) + x * c
+    barrier = pltpu.get_barrier_semaphore()
+    for p in peers:
+        pl.semaphore_signal(barrier, inc=1, device_id=p, device_id_type=MESH)
+    units = [(gq, oq, 0, i) for i in range(3)] + [(go, oo, 0, 0)]
+    units = [(gd, od, i, 0) for i in range(4)] + [(gu, ou, 0, i) for i in range(4)] + [(go, oo, 0, 0)] + [(gq, oq, 0, i) for i in range(3)]
+    n_units = len(units)
+    W, H = 768, 384
+    mine = pl.ds(pl.multiple_of(c * H, 128), H)
+    other = pl.ds(pl.multiple_of((1 - c) * H, 128), H)
+
+    def block(ref, i, j):
+        return ref.at[pl.ds(i * W, W), pl.ds(j * W, W)]
+
+    loads = []
+    for u, (src, _, i, j) in enumerate(units):
+        cp = pltpu.make_async_copy(block(src, i, j), own.at[u], lsem.at[u])
+        cp.start()
+        loads.append(cp)
+    pl.semaphore_wait(barrier, len(peers))
+
+    def remote(src, dst, u, k, dev):
+        cp = pltpu.make_async_remote_copy(src_ref=src, dst_ref=dst, send_sem=ss.at[u, k], recv_sem=rs.at[u, k], device_id=dev, device_id_type=MESH)
+        cp.start()
+        return cp
+
+    def rows(start, size):
+        return pl.ds(pl.multiple_of(start, 16), size)
+
+    def add_rows(dst, dst_at, a, a_at, b, b_at, n, step):
+        @pl.loop(0, n, step=step)
+        def _(t):
+            s = a(a_at + t, step).astype(jnp.float32) + b(b_at + t, step).astype(jnp.float32)
+            dst(dst_at + t, step, s.astype(jnp.bfloat16))
+
+    pend = {}
+    base1 = b1 * 384
+    base2 = b1 * 384 + b2 * 192
+    base3 = base2 + z * 48
+
+    def step(u, s):
+        if s == 0:
+            loads[u].wait()
+            pend[u, 0] = remote(own.at[u, :, other], r0.at[u], u, 0, core_dev)
+        elif s == 1:
+            pend[u, 0].wait_recv()
+
+            @pl.loop(0, 768, step=64)
+            def _(t):
+                q = pl.ds(pl.multiple_of(t, 64), 64)
+                r0[u, q, :] = (r0[u, q, :].astype(jnp.float32) + own[u, q, mine].astype(jnp.float32)).astype(jnp.bfloat16)
+
+            pend[u, 1] = remote(r0.at[u, rows((1 - b1) * 384, 384), :], r1.at[u], u, 1, d1_dev)
+        elif s == 2:
+            pend[u, 1].wait_recv()
+
+            @pl.loop(0, 384, step=64)
+            def _(t):
+                q = pl.ds(pl.multiple_of(t, 64), 64)
+                r1[u, q, :] = (r1[u, q, :].astype(jnp.float32) + r0[u, rows(base1 + t, 64), :].astype(jnp.float32)).astype(jnp.bfloat16)
+
+            pend[u, 2] = remote(r1.at[u, rows((1 - b2) * 192, 192), :], r2.at[u], u, 2, d2_dev)
+        elif s == 3:
+            pend[u, 2].wait_recv()
+
+            @pl.loop(0, 192, step=64)
+            def _(t):
+                q = pl.ds(pl.multiple_of(t, 64), 64)
+                r2[u, q, :] = (r2[u, q, :].astype(jnp.float32) + r1[u, rows(b2 * 192 + t, 64), :].astype(jnp.float32)).astype(jnp.bfloat16)
+
+            for k in range(3):
+                zz = lax.rem(z + k + 1, 4)
+                pend[u, 3 + k] = remote(r2.at[u, rows(zz * 48, 48), :], r3.at[u, k], u, 3 + k, z_devs[k])
+        elif s == 4:
+            for k in range(3):
+                pend[u, 3 + k].wait_recv()
+            tot = r2[u, rows(z * 48, 48), :].astype(jnp.float32)
+            for k in range(3):
+                tot = tot + r3[u, k].astype(jnp.float32)
+            out[u, rows(base3, 48), mine] = tot.astype(jnp.bfloat16)
+            region = out.at[u, rows(base3, 48), mine]
+            for k in range(3):
+                pend[u, 6 + k] = remote(region, region, u, 6 + k, z_devs[k])
+        elif s == 5:
+            for k in range(3):
+                pend[u, 6 + k].wait_recv()
+            region = out.at[u, rows(base2, 192), mine]
+            pend[u, 9] = remote(region, region, u, 9, d2_dev)
+        elif s == 6:
+            pend[u, 9].wait_recv()
+            region = out.at[u, rows(base1, 384), mine]
+            pend[u, 10] = remote(region, region, u, 10, d1_dev)
+        elif s == 7:
+            pend[u, 10].wait_recv()
+            region = out.at[u, :, mine]
+            pend[u, 11] = remote(region, region, u, 11, core_dev)
+        elif s == 8:
+            pend[u, 11].wait_recv()
+            _, dst, i, j = units[u]
+            cp = pltpu.make_async_copy(out.at[u], block(dst, i, j), osem.at[u])
+            cp.start()
+            pend[u, 12] = cp
+
+    small = {}
+    small_devs = [core_dev, d1_dev, d2_dev, (lax.rem(z + 2, 4) * 2 + x, r_ax), ((z + 1 - 2 * lax.rem(z, 2)) * 2 + x, r_ax)]
+
+    def small_step(k):
+        if k == 0:
+            smr[0] = sm[...]
+        else:
+            small[k - 1].wait_recv()
+            smr[k] = smr[k - 1] + smr[k + 5]
+        if k < 5:
+            small[k] = pltpu.make_async_remote_copy(src_ref=smr.at[k], dst_ref=smr.at[k + 6], send_sem=sss.at[k], recv_sem=srs.at[k], device_id=small_devs[k], device_id_type=MESH)
+            small[k].start()
+        else:
+            osm[...] = smr[5]
+
+    for tau in range(n_units + 8):
+        for s in range(8, -1, -1):
+            u = tau - s
+            if 0 <= u < n_units:
+                step(u, s)
+        if tau < 6:
+            small_step(tau)
+    for u in range(n_units):
+        for k in range(12):
+            pend[u, k].wait_send()
+        pend[u, 12].wait()
+    for k in range(5):
+        small[k].wait_send()
+
+
+def weight_sums(gq, go, gu, gd, sm):
+    n = 12
+    bf = jnp.bfloat16
+    return pl.pallas_call(
+        functools.partial(wsum_kernel, None),
+        out_shape=(
+            jax.ShapeDtypeStruct(gq.shape, bf),
+            jax.ShapeDtypeStruct(go.shape, bf),
+            jax.ShapeDtypeStruct(gu.shape, bf),
+            jax.ShapeDtypeStruct(gd.shape, bf),
+            jax.ShapeDtypeStruct(sm.shape, sm.dtype),
+        ),
+        in_specs=[pl.BlockSpec(memory_space=pl.ANY)] * 4 + [pl.BlockSpec(memory_space=pltpu.VMEM)],
+        out_specs=[pl.BlockSpec(memory_space=pl.ANY)] * 4 + [pl.BlockSpec(memory_space=pltpu.VMEM)],
+        scratch_shapes=[
+            pltpu.VMEM((n, 768, 768), bf),
+            pltpu.VMEM((n, 768, 768), bf),
+            pltpu.VMEM((n, 768, 384), bf),
+            pltpu.VMEM((n, 384, 384), bf),
+            pltpu.VMEM((n, 192, 384), bf),
+            pltpu.VMEM((n, 3, 48, 384), bf),
+            pltpu.VMEM((11,) + sm.shape, jnp.float32),
+            pltpu.SemaphoreType.DMA((n,)),
+            pltpu.SemaphoreType.DMA((n,)),
+            pltpu.SemaphoreType.DMA((n, 12)),
+            pltpu.SemaphoreType.DMA((n, 12)),
+            pltpu.SemaphoreType.DMA((5,)),
+            pltpu.SemaphoreType.DMA((5,)),
+        ],
+        compiler_params=pltpu.CompilerParams(collective_id=10, has_side_effects=True, vmem_limit_bytes=60 * 2**20),
+        name="weight_sums",
+    )(gq, go, gu, gd, sm)
 
 
 def on_device(
@@ -305,6 +489,25 @@
         delta_joined, w_qkv.T, preferred_element_type=jnp.float32
     )
     norm_terms = jnp.stack([delta_gain1, delta_bias1, delta_gain2, delta_bias2])
+    if lax.axis_size("seq") == 8 and lax.axis_size("row") == 4:
+        bf = jnp.bfloat16
+        taps_row = jnp.pad(grad_taps.reshape(1, -1), ((0, 3), (0, model_width - grad_taps.size)))
+        sm = jnp.concatenate([norm_terms, taps_row], axis=0)
+        tq, to, tu, td, tsm = weight_sums(grad_joined.astype(bf), grad_output.astype(bf), grad_up.astype(bf), grad_down.astype(bf), sm)
+        f32 = jnp.float32
+        return (
+            result.astype(jnp.bfloat16)[None],
+            delta_inputs[None],
+            tq.astype(f32),
+            to.astype(f32),
+            tsm[4, : grad_taps.size].reshape(grad_taps.shape),
+            tsm[0],
+            tsm[1],
+            tu.astype(f32),
+            td.astype(f32),
+            tsm[2],
+            tsm[3],
+        )
     taps_total, norms_total = lax.psum((grad_taps, norm_terms), ("seq", "row"))
     groups = lax.axis_size(("seq", "row"))
     summed = (

time: 1970 us -> 1210 us (0.61)
  blocking collectives: 528 us -> 69.5 us
  waiting for transfers between devices: 301 us -> 59.5 us
  Pallas kernels: 0 us -> 143 us
  other arithmetic: 375 us -> 241 us
  local copies, waits for them, and re-layouts: 313 us -> 245 us
    unnamed x1 -> x0, blocking collectives: 459 us -> none
    all_gather x4 -> x0, waiting for transfers between devices: 151 us -> none  [the longest x1 62.1 us: on_device(): lax.all_gather(summed[0].astype(jnp.bfloat16), ('seq', 'row'), axis=0, ti...]
    pallas_call x0 -> x1, Pallas kernels: none -> 143 us  [weight_sums(): pl.pallas_call(functools.partial(wsum_kernel, None), out_shape=(jax.Shape...]
    reshape x4 -> x0, other arithmetic: 140 us -> none  [the longest x1 65.8 us: on_device(): gathered[0].reshape(grad_joined.shape)]
    psum x2, waiting for transfers between devices: 72.5 us -> 21.5 us  [on_device(): lax.psum((carried_part, keymark_part.reshape(slot_count, model_width)), '...]
    reshape x8 -> x1, local copies, waits for them, and re-layouts: 51.4 us -> 0.67 us  [on_device(): grad_taps.reshape(1, -1)]
    psum x1, waiting for transfers between devices: 60.2 us -> 26.6 us  [on_device(): lax.psum((jnp.sum(exponent, axis=2), weighted_part), 'seq')]
    unnamed x347 -> x354, local copies, waits for them, and re-layouts: 86.8 us -> 72.5 us
  transfers between devices with their start and end apart: 12 -> 8, of which waited for: 8 -> 3; matrix products, arithmetic and copies ran while one was open for 24% -> 30% of each run, Pallas kernels for 0% -> 0%
where the time goes in v1:
time: 1210 us; the launch traced here: 1200 us
  matrix products  416 us (34%)
  local copies, waits for them, and re-layouts  245 us (20%)
  other arithmetic  241 us (20%)
  Pallas kernels  143 us (12%)
  blocking collectives  69.5 us (6%)
  waiting for transfers between devices  59.5 us (5%)
  between operations  16.4 us (1%)
    pallas_call x1, Pallas kernels, weight_sums(): pl.pallas_call(functools.partial(wsum_kernel, None), out_shape=(jax.Shape...  143 us
    dot_general x36, matrix products, inverse_from_scores(): jnp.einsum('dhlm,dhmn->dhln', product, bracket, precision=HIGHEST)  90.6 us
    unnamed x354, local copies, waits for them, and re-layouts  72.5 us
    dot_general x18, matrix products, inverse_from_scores(): product = jnp.einsum('dhlm,dhmn->dhln', kernel_a, approx, precision=HIGHEST)  61.1 us
    another operation x3, other arithmetic  59.5 us
    convert_element_type x1, other arithmetic, on_device(): mixture_b = (attended + convolved).astype(jnp.bfloat16)  59.4 us
    reduce_sum x7, other arithmetic, on_device(): jnp.sum(jnp.where(same_doc, delta_mixture * padded[tap_index:tap_index +...  59.3 us
    dot_general x18, matrix products, inverse_from_scores(): jnp.einsum('dhlm,dhmn->dhln', approx, bracket, precision=HIGHEST)  47 us
  transfers between devices with their start and end apart: 8, of which 3 were waited for; matrix products, arithmetic and copies ran while one was open for 30% of the time, Pallas kernels for 0%

profile of v1, /device:TPU:0, one launch (start us, length us, event | category | flops | bytes accessed | tf_op | source)
XLA Modules:
  0.0 1202.2 jit_solution(10805571905079724302)
XLA Ops:
  100.8 11.3 all-reduce.7.cloned.1.call-done
  190.8 7.4 select_reduce_fusion
  198.1 35.5 %pmax.7 = f32[12,256]{1,0:T(8,128)S(1)} all-reduce(f32[12,256]{1,0:T(8,128)} %get-tuple-element.205), channel_id=1, replica_groups=mesh['seq'=8,'row'=4] {'seq'}, use_global_device_ids=true, to_apply=%region_7.8 | all-reduce | flops 3072 | bytes 24576 | tf_op jit(solution)/shard_map/pmax | solution.py:334
  233.7 7.9 fusion.8
  247.2 33.9 %psum.44 = f32[256,12]{0,1:T(8,128)S(1)} all-reduce(f32[256,12]{0,1:T(8,128)} %bitcast.326), channel_id=1, replica_groups=mesh['seq'=8,'row'=4] {'seq'}, use_global_device_ids=true, to_apply=%region_10.11 | all-reduce | flops 3072 | bytes 24576 | tf_op jit(solution)/shard_map/psum | solution.py:340
  281.2 11.7 fusion.381
  292.9 26.6 %all-reduce.9.cloned.1.call-done = f32[256,12,64]{0,2,1:T(8,128)} async-done(((f32[256,12,64]{0,2,1:T(8,128)}), f32[256,12,64]{0,2,1:T(8,128)}) %all-reduce.9.cloned.1.call-update) | async-done | bytes 786448 | tf_op jit(solution)/shard_map/psum | solution.py:340
  335.6 7.5 fusion.226
  346.7 59.4 %fusion.128 = bf16[1024,768]{1,0:T(8,128)(2,1)} fusion(f32[1024,768]{1,0:T(8,128)} %copy.234, bf16[1024,768]{1,0:T(8,128)(2,1)} %get-tuple-element.160, bf16[16,768]{1,0:T(8,128)(2,1)} %collective-permute-done.1, bf16[16,768]{1,0:T(8,128)(2,1)} %collective-permute-done, f32[768]{0:T(1024)} %broadcast_in_dim.924, f32[768]{0:T(1024)} %broadcast_in_dim.921, ...), kind=kLoop, calls=%fused_computation.244 | loop fusion | flops 180092928 | bytes 6475776 | tf_op jit(solution)/shard_map/convert_element_type | solution.py:368
  410.8 12.4 %multiply_convert_fusion.1 = (bf16[1024,3072]{1,0:T(8,128)(2,1)}, f32[1024,3072]{1,0:T(8,128)}) fusion(bf16[768,3072]{1,0:T(8,128)(2,1)} %param.19, f32[1024,768]{0,1:T(8,128)S(1)} %get-tuple-element.212, f32[768]{0:T(1024)S(1)} %copy-done.148, f32[768]{0:T(1024)S(1)} %copy-done.140, f32[1024]{0:T(1024)S(1)} %fusion.349, f32[1024]{0:T(1024)S(1)} %broadcast_multiply_fusion.1), kind=kOutput, calls=%fused_computation.12 | convolution fusion | flops 4851499008 | bytes 26753024 | tf_op jit(solution)/shard_map/dot_general | solution.py:374
  423.2 8.0 fusion.383
  435.6 7.8 convolution_convert_fusion.1.gd
  443.4 13.2 %add_convert_fusion = bf16[1024,3072]{1,0:T(8,128)(2,1)} fusion(f32[1024,3072]{1,0:T(8,128)} %get-tuple-element.214, bf16[3072,768]{1,0:T(8,128)(2,1)S(1)} %bitcast.330, f32[1024]{0:T(1024)S(1)} %negate_multiply_fusion.1, bf16[1,1024,768]{1,2,0:T(8,128)(2,1)S(1)} %copy-done.25, f32[1024,768]{0,1:T(8,128)S(1)} %get-tuple-element.216, ...), kind=kOutput, calls=%fused_computation.11 | convolution fusion | flops 4879810560 | bytes 28331008 | tf_op jit(solution)/shard_map/dot_general | solution.py:382
  456.6 9.4 multiply_reduce_fusion
  466.0 10.2 convolution_convert_fusion.2.gu
  478.1 8.0 fusion.139
  488.6 8.1 fusion.311
  496.7 9.0 fusion.1
  505.8 6.9 fusion.3
  527.0 8.6 fusion.66
  541.0 7.9 fusion.78
  554.3 8.4 fusion.90
  568.0 10.3 fusion.151
  579.6 10.2 fusion.105
  595.2 9.6 fusion.117
  693.1 21.5 %all-reduce.11.cloned.1.call-done = f32[4,64,12,64]{3,1,2,0:T(8,128)} async-done(((f32[4,64,12,64]{3,1,2,0:T(8,128)}), f32[4,64,12,64]{3,1,2,0:T(8,128)}) %all-reduce.11.cloned.1.call-update) | async-done | bytes 786448 | tf_op jit(solution)/shard_map/psum | solution.py:433
  855.8 8.0 fusion.358
  880.4 13.6 %multiply_convert_fusion = bf16[12,256,1024]{2,1,0:T(8,128)(2,1)} fusion(f32[12,256,1024]{2,1,0:T(8,128)} %fusion.358, f32[12,256,1024]{2,1,0:T(8,128)} %get-tuple-element.206, f32[12,256]{1,0:T(8,128)S(1)} %bitcast.325, f32[12,256]{1,0:T(8,128)S(1)} %copy-done.107, pred[256,1024]{1,0:T(8,128)(4,1)S(1)} %copy-done.81, ...), kind=kOutput, calls=%fused_computation.10 | convolution fusion | flops 425656320 | bytes 34115584 | tf_op jit(solution)/shard_map/the,she->hst/dot_general | solution.py:458
  907.7 57.4 %fusion.156 = bf16[1024,768]{1,0:T(8,128)(2,1)} fusion(f32[1024,768]{1,0:T(8,128)} %copy.273, f32[1056,768]{1,0:T(8,128)} %maximum_convert_fusion, f32[768]{0:T(1024)} %broadcast_in_dim.924, f32[768]{0:T(1024)} %broadcast_in_dim.921, f32[768]{0:T(1024)} %broadcast_in_dim.918, f32[768]{0:T(1024)} %broadcast_in_dim.915, f32[768]{0:T(1024)} %broadcast_in_dim.912, ...), kind=kLoop, calls=%fused_computation.273 | loop fusion | flops 78643200 | bytes 108662784 | tf_op jit(solution)/shard_map/convert.2
  965.0 10.5 multiply_reduce_fusion.4
  1021.8 143.5 %weight_sums.1 = (bf16[768,2304]{1,0:T(8,128)(2,1)}, bf16[768,768]{1,0:T(8,128)(2,1)}, bf16[768,3072]{1,0:T(8,128)(2,1)}, bf16[3072,768]{1,0:T(8,128)(2,1)}, f32[8,768]{1,0:T(8,128)}) custom-call(bf16[768,2304]{1,0:T(8,128)(2,1)} %fusion.13.gq, bf16[768,768]{1,0:T(8,128)(2,1)} %convolution_convert_fusion.4.go, ...), custom_call_target="tpu_custom_call" | custom-call | tf_op jit(solution)/shard_map/weight_sums/pallas_call | solution.py:245
  1167.5 8.9 add_bitcast_fusion
  (657 shorter events, 573.1 us)
Async XLA Ops:
  7.2 104.9 %all-reduce.7.cloned.1.call-start = ((), (), s32[]{:S(2)}) async-start(), calls=%async_computation | async-start | bytes 3145728 | tf_op jit(solution)/shard_map/psum | solution.py:314
  20.2 299.3 %all-reduce.9.cloned.1.call-start = ((), (), s32[]{:S(2)}) async-start(), calls=%async_computation.1 | async-start | bytes 1572864 | tf_op jit(solution)/shard_map/psum | solution.py:340
  21.6 325.0 %collective-permute-start = (bf16[16,768]{1,0:T(8,128)(2,1)}, bf16[16,768]{1,0:T(8,128)(2,1)}, u32[]{:S(2)}, u32[]{:S(2)}) collective-permute-start(bf16[16,768]{1,0:T(8,128)(2,1)} %get-tuple-element.156), channel_id=1, source_target_pairs={{0,4},{4,8},{8,12},{12,16},{16,20},{20,24},{24,28},{1,5},{5,9},{9,... | collective-permute-start | bytes 73736 | tf_op jit(solution)/shard_map/ppermute | solution.py:29
  27.1 319.6 %collective-permute-start.1 = (bf16[16,768]{1,0:T(8,128)(2,1)}, bf16[16,768]{1,0:T(8,128)(2,1)}, u32[]{:S(2)}, u32[]{:S(2)}) collective-permute-start(bf16[16,768]{1,0:T(8,128)(2,1)} %get-tuple-element.157), channel_id=1, source_target_pairs={{4,0},{8,4},{12,8},{16,12},{20,16},{24,20},{28,24},{5,1},{9,5},{13... | collective-permute-start | bytes 73736 | tf_op jit(solution)/shard_map/ppermute | solution.py:30
  28.4 10.6 copy-start.130
  97.5 17.2 %copy-start.128 = (f32[256]{0:T(256)}, f32[256]{0:T(256)S(1)}, u32[]{:S(2)}) copy-start(f32[256]{0:T(256)S(1)} %subtract_convert_fusion.1) | copy-start | bytes 3076
  125.6 55.5 %copy-start.22 = (f32[4,12,64,64]{2,3,1,0:T(8,128)}, f32[4,12,64,64]{2,3,1,0:T(8,128)S(1)}, u32[]{:S(2)}) copy-start(f32[4,12,64,64]{2,3,1,0:T(8,128)S(1)} %get-tuple-element.208) | copy-start | bytes 2359300
  125.6 55.5 %copy-start.98 = (f32[4,12,64]{2,1,0:T(8,128)}, f32[4,12,64]{2,1,0:T(8,128)S(1)}, u32[]{:S(2)}) copy-start(f32[4,12,64]{2,1,0:T(8,128)S(1)} %get-tuple-element.207) | copy-start | bytes 36868
  127.7 53.4 %copy-start.101 = (f32[4,12,64]{2,1,0:T(8,128)}, f32[4,12,64]{2,1,0:T(8,128)S(1)}, u32[]{:S(2)}) copy-start(f32[4,12,64]{2,1,0:T(8,128)S(1)} %get-tuple-element.163) | copy-start | bytes 36868
  233.7 10.6 copy-start.20
  247.2 467.4 %all-reduce.11.cloned.1.call-start = ((), (), s32[]{:S(2)}) async-start(), calls=%async_computation.2 | async-start | bytes 3145728 | tf_op jit(solution)/shard_map/psum | solution.py:433
  281.2 38.3 %copy-start.95 = (f32[256,12]{0,1:T(8,128)}, f32[256,12]{0,1:T(8,128)S(1)}, u32[]{:S(2)}) copy-start(f32[256,12]{0,1:T(8,128)S(1)} %psum.44) | copy-start | bytes 36868
  406.1 17.1 %slice-start.5 = ((s8[4718592]{0:T(1024)(128)(4,1)}), s8[4194304]{0:T(1024)(128)(4,1)S(1)}, s32[]{:S(2)}) async-start(s8[4718592]{0:T(1024)(128)(4,1)} %bitcast.329), calls=%async_computation.9 | async-start | bytes 8388608
  410.8 12.4 %slice-start.6 = ((s8[4718592]{0:T(1024)(128)(4,1)}), s8[524288]{0:T(1024)(128)(4,1)S(1)}, s32[]{:S(2)}) async-start(s8[4718592]{0:T(1024)(128)(4,1)} %bitcast.329), calls=%async_computation.10 | async-start | bytes 1048576
  435.6 21.0 %slice-start.7 = ((s8[4718592]{0:T(1024)(128)(4,1)}), s8[4194304]{0:T(1024)(128)(4,1)S(1)}, s32[]{:S(2)}) async-start(s8[4718592]{0:T(1024)(128)(4,1)} %bitcast.331), calls=%async_computation.11 | async-start | bytes 8388608
  443.4 13.2 %slice-start.8 = ((s8[4718592]{0:T(1024)(128)(4,1)}), s8[524288]{0:T(1024)(128)(4,1)S(1)}, s32[]{:S(2)}) async-start(s8[4718592]{0:T(1024)(128)(4,1)} %bitcast.331), calls=%async_computation.12 | async-start | bytes 1048576
  477.2 8.9 copy-start.85
  477.2 8.8 copy-start.141
  488.6 8.1 copy-start.104
  488.6 8.1 copy-start.111
  488.6 17.1 %slice-start.2 = ((s8[12582912]{0:T(1024)(128)(4,1)}), s8[4194304]{0:T(1024)(128)(4,1)S(1)}, s32[]{:S(2)}) async-start(s8[12582912]{0:T(1024)(128)(4,1)} %bitcast.309), calls=%async_computation.6 | async-start | bytes 8388608
  488.6 17.1 %slice-start.3 = ((s8[12582912]{0:T(1024)(128)(4,1)}), s8[4194304]{0:T(1024)(128)(4,1)S(1)}, s32[]{:S(2)}) async-start(s8[12582912]{0:T(1024)(128)(4,1)} %bitcast.309), calls=%async_computation.7 | async-start | bytes 8388608
  496.7 9.0 slice-start.4
  626.4 381.6 %all-reduce.13.cloned.1.call-start = ((), (), s32[]{:S(2)}) async-start(), calls=%async_computation.3 | async-start | bytes 3145728 | tf_op jit(solution)/shard_map/psum | solution.py:433
  626.4 63.3 %collective-permute-start.2 = (bf16[16,768]{1,0:T(8,128)(2,1)}, bf16[16,768]{1,0:T(8,128)(2,1)}, u32[]{:S(2)}, u32[]{:S(2)}) collective-permute-start(bf16[16,768]{1,0:T(8,128)(2,1)} %get-tuple-element.164), channel_id=1, source_target_pairs={{0,4},{4,8},{8,12},{12,16},{16,20},{20,24},{24,28},{1,5},{5,9},{9,... | collective-permute-start | bytes 73736 | tf_op jit(solution)/shard_map/ppermute | solution.py:29
  629.5 60.2 %collective-permute-start.3 = (bf16[16,768]{1,0:T(8,128)(2,1)}, bf16[16,768]{1,0:T(8,128)(2,1)}, u32[]{:S(2)}, u32[]{:S(2)}) collective-permute-start(bf16[16,768]{1,0:T(8,128)(2,1)} %get-tuple-element.165), channel_id=1, source_target_pairs={{4,0},{8,4},{12,8},{16,12},{20,16},{24,20},{28,24},{5,1},{9,5},{13... | collective-permute-start | bytes 73736 | tf_op jit(solution)/shard_map/ppermute | solution.py:30
  669.5 11.9 copy-start.122
  875.4 24.9 %slice-start = ((s8[6291456]{0:T(1024)(128)(4,1)}), s8[4194304]{0:T(1024)(128)(4,1)S(1)}, s32[]{:S(2)}) async-start(s8[6291456]{0:T(1024)(128)(4,1)} %bitcast.299), calls=%async_computation.4 | async-start | bytes 8388608
  880.4 19.9 %slice-start.1 = ((s8[6291456]{0:T(1024)(128)(4,1)}), s8[2097152]{0:T(1024)(128)(4,1)S(1)}, s32[]{:S(2)}) async-start(s8[6291456]{0:T(1024)(128)(4,1)} %bitcast.299), calls=%async_computation.5 | async-start | bytes 4194304
  965.0 10.5 copy-start.66
  1021.8 145.7 %copy-start.142 = (f32[1024]{0:T(1024)S(1)}, f32[1024]{0:T(1024)}, u32[]{:S(2)}) copy-start(f32[1024]{0:T(1024)} %copy-done.141) | copy-start | bytes 12292
  1167.5 8.9 copy-start.79
  (135 other events, 431.9 us)
Sparse Core Ops, SparseCore 0:
  20.3 91.7 all-reduce.6
  247.3 72.1 all-reduce.8
  626.5 88.0 all-reduce.10
  907.1 88.7 all-reduce.12
